TPU v7x, 512 devices: a whole 4x4x16 slice. The times are simulated.
512 devices in a mesh: band: 8 (over x, core), pw: 64 (over z, y).
Axes of the slice: x: 4, y: 4, z: 16, core: 2. Of those that a mesh axis runs over, the one named last changes fastest.
Arguments:
- orbital_coefficients: float32 [8, 2, 128, 128, 128], P('band', None, 'pw'), may hold values from -6 to 6
- sphere_halfwidth: int32 [128, 128], P('pw'), may hold values from -1 to 63, as said below
- occupation: float32 [8], P('band'), may hold values from 0.5 to 2
- local_potential: float32 [256, 256, 256], P(None, 'pw'), may hold values from -6 to 6
- stencil_corner: int32 [64, 64, 128], P('pw'), may hold values from 0 to 262143, as said below
- stencil_weight: float32 [8, 64, 64, 128], P(None, 'pw'), may hold values from -3 to 3
- point_count: int32 [64, 64], P('pw'), may hold values from 0 to 128, as said below
Outputs:
- local_action: float32 [8, 2, 128, 128, 128], P('band', None, 'pw')
- fit_potential: float32 [64, 64, 128], P('pw')
Inputs may be any that keep to these rules, and one draw needn't show every extreme that they name: `sphere_halfwidth`: in every draw the kept columns form one sphere centred at frequency zero that reaches the cube's faces; -1 marks an empty column. `stencil_corner`: each corner is x * 4 + y times 256 plus z, with x and z in 0 to 255 and y in 0 to 3. `point_count`: in every draw some tile has all 128 slots live from every source, and every source has some block with all 128 slots live.
All inputs are finite; a program needn't handle non-finite values.
Results may differ from a plain program's by a relative error of at most 0.0003.
Values sent between devices are 32-bit elements; how exact they have to be, the bound alone decides.
A program may use at most 64 MiB of HBM per device.

v0:
```python
import math
import jax
import jax.numpy as jnp
from jax import lax
from jax.sharding import PartitionSpec as P

hartree_scale = 200.0
exact_mode = lax.Precision.HIGHEST


def shifted(value, axis, steps):
    count = lax.axis_size(axis)
    pairs = [(source, (source + steps) % count) for source in range(count)]
    return lax.ppermute(value, axis, pairs)


def phases(frequency, grid_size):
    position = jnp.arange(grid_size, dtype=jnp.int32)
    product = jnp.remainder(frequency[:, None] * position[None, :], grid_size)
    angle = product.astype(jnp.float32) * (2.0 * math.pi / grid_size)
    return (jnp.cos(angle), jnp.sin(angle))


def inverse_table(frequency, grid_size):
    cosine, sine = phases(frequency, grid_size)
    from_real = jnp.stack([cosine, sine], axis=1)
    from_imag = jnp.stack([-sine, cosine], axis=1)
    return jnp.stack([from_real, from_imag], axis=0)


def forward_table(frequency, grid_size):
    cosine, sine = phases(frequency, grid_size)
    from_real = jnp.stack([cosine.T, -sine.T], axis=1)
    from_imag = jnp.stack([sine.T, cosine.T], axis=1)
    return jnp.stack([from_real, from_imag], axis=0)


def transform(operand, matrix, target_axis, component_axis):
    result = lax.dot_general(
        operand,
        matrix,
        (((component_axis, target_axis), (0, 1)), ((), ())),
        precision=exact_mode,
        preferred_element_type=jnp.float32,
    )
    dimensions = operand.ndim
    return jnp.moveaxis(result, (dimensions - 2, dimensions - 1), (component_axis, target_axis))


def kernel_values(start_x, count_x, start_y, count_y, grid_size):

    def signed(start, count):
        frequency = start + jnp.arange(count, dtype=jnp.int32)
        return jnp.where(frequency < grid_size // 2, frequency, frequency - grid_size)

    along_x = signed(start_x, count_x)
    along_y = signed(start_y, count_y)
    along_z = signed(0, grid_size)
    square = along_x[:, None, None] ** 2 + along_y[None, :, None] ** 2 + along_z[None, None, :] ** 2
    return jnp.where(square > 0, hartree_scale / jnp.maximum(square, 1).astype(jnp.float32), 0.0)


def body(
    orbital_coefficients,
    sphere_halfwidth,
    occupation,
    local_potential,
    stencil_corner,
    stencil_weight,
    point_count,
):
    cube_size = orbital_coefficients.shape[3]
    grid_size = local_potential.shape[0]
    slab_depth = local_potential.shape[1]
    slot_count = stencil_corner.shape[2]
    cube_freq = jnp.arange(cube_size, dtype=jnp.int32) - cube_size // 2
    sphere_mask = (jnp.abs(cube_freq)[None, None, :] <= sphere_halfwidth[:, :, None]).astype(
        jnp.float32
    )
    scale_in = float(cube_size) ** (-1.5)
    scale_out = float(cube_size) ** 1.5 / float(grid_size) ** 3
    inverse_cube = inverse_table(cube_freq, grid_size)
    forward_cube = forward_table(cube_freq, grid_size)
    coefficient = orbital_coefficients * (sphere_mask * scale_in)[None, None]
    partial_section = transform(coefficient, inverse_cube, 4, 1)
    partial_section = transform(partial_section, inverse_cube, 3, 1)
    orbital = transform(
        lax.all_to_all(partial_section, "pw", split_axis=3, concat_axis=2, tiled=True),
        inverse_cube,
        2,
        1,
    )
    partial_density = jnp.sum(
        occupation[:, None, None, None] * (orbital[:, 0] ** 2 + orbital[:, 1] ** 2), axis=0
    )
    product = orbital * local_potential[None, None]
    forward_section = transform(product, forward_cube, 2, 1)
    pencil = lax.all_to_all(forward_section, "pw", split_axis=2, concat_axis=3, tiled=True)
    pencil = transform(pencil, forward_cube, 3, 1)
    spectrum_cube = transform(pencil, forward_cube, 4, 1)
    local_action = spectrum_cube * (sphere_mask * scale_out)[None, None]
    grid_freq = jnp.arange(grid_size, dtype=jnp.int32)
    forward_grid = forward_table(grid_freq, grid_size)
    inverse_grid = inverse_table(grid_freq, grid_size)
    pw_count = lax.axis_size("pw")
    band_count = lax.axis_size("band")
    x_block = grid_size // pw_count
    x_start = lax.axis_index("pw") * x_block
    inverse_norm = 1.0 / float(grid_size) ** 3
    y_block = grid_size // band_count
    y_start = lax.axis_index("band") * y_block
    density_part = lax.psum_scatter(partial_density, "band", scatter_dimension=2, tiled=True)
    spectrum = transform(density_part[None], forward_grid[0:1], 1, 0)
    spectrum = lax.all_to_all(spectrum, "pw", split_axis=1, concat_axis=2, tiled=True)
    spectrum = transform(spectrum, forward_grid, 2, 0)
    spectrum = lax.all_to_all(spectrum, "band", split_axis=2, concat_axis=3, tiled=True)
    spectrum = transform(spectrum, forward_grid, 3, 0)
    spectrum = spectrum * kernel_values(x_start, x_block, y_start, y_block, grid_size)[None]
    spectrum = transform(spectrum, inverse_grid, 3, 0)
    spectrum = lax.all_to_all(spectrum, "band", split_axis=3, concat_axis=2, tiled=True)
    spectrum = transform(spectrum, inverse_grid, 2, 0)
    spectrum = lax.all_to_all(spectrum, "pw", split_axis=2, concat_axis=1, tiled=True)
    hartree_part = transform(spectrum, inverse_grid[:, :, 0:1], 1, 0)[0] * inverse_norm
    hartree = lax.all_gather(hartree_part, "band", axis=2, tiled=True)
    upper_plane = shifted(hartree[:, 0:1, :], "pw", -1)
    extended = jnp.concatenate([hartree, upper_plane], axis=1)
    flattened = extended.reshape(-1)
    plane_cells = slab_depth * grid_size
    request = lax.all_to_all(stencil_corner, "pw", split_axis=1, concat_axis=0, tiled=True)
    coord_x = request // plane_cells
    coord_y = request // grid_size % slab_depth
    coord_z = request % grid_size
    gathered = []
    for corner in range(8):
        step_x = corner // 4
        step_y = corner // 2 % 2
        step_z = corner % 2
        cell_index = (
            (coord_x + step_x) % grid_size * (slab_depth + 1) + coord_y + step_y
        ) * grid_size + (coord_z + step_z) % grid_size
        gathered.append(flattened[cell_index])
    stacked = jnp.stack(gathered, axis=0)
    sampled = lax.all_to_all(stacked, "pw", split_axis=1, concat_axis=2, tiled=True)
    summed = jnp.sum(stencil_weight * sampled, axis=0)
    live_slot = jnp.arange(slot_count, dtype=jnp.int32)[None, None, :] < point_count[:, :, None]
    fit_potential = jnp.where(live_slot, summed, 0.0)
    return (local_action, fit_potential)


def solution(mesh):
    placed = (
        P("band", None, "pw", None, None),
        P("pw", None),
        P("band"),
        P(None, "pw", None),
        P("pw", None, None),
        P(None, "pw", None, None),
        P("pw", None),
    )
    return jax.shard_map(
        body,
        mesh=mesh,
        in_specs=placed,
        out_specs=(P("band", None, "pw", None, None), P("pw", None, None)),
        check_vma=False,
    )
```

profile of v0, /device:TPU:8, one launch (start us, length us, event | category | flops | bytes accessed | tf_op | source)
XLA Modules:
  0.0 736.5 jit_solution(2443056056476492475)
XLA Ops:
  10.3 1.3 copy.52
  11.6 18.7 %all-to-all-start = ((f32[1,2,2,256,256]{4,1,2,0,3:T(2,128)}), f32[1,2,2,256,256]{4,1,2,0,3:T(2,128)S(1)}, u32[]{:S(2)}, u32[]{:S(2)}) async-start(f32[1,2,2,256,256]{4,1,2,0,3:T(2,128)} %copy.52), calls=%async_computation | async-start | bytes 2097152 | tf_op jit(solution)/shard_map/all_to_all | solution.py:88
  31.1 54.5 %all-to-all-done = f32[1,2,2,256,256]{4,1,2,0,3:T(2,128)S(1)} async-done(((f32[1,2,2,256,256]{4,1,2,0,3:T(2,128)}), f32[1,2,2,256,256]{4,1,2,0,3:T(2,128)S(1)}, u32[]{:S(2)}, u32[]{:S(2)}) %all-to-all-start) | async-done | bytes 1048608 | tf_op jit(solution)/shard_map/all_to_all | solution.py:88
  86.4 1.9 convolution_bitcast_fusion
  88.3 1.1 fusion.14
  91.4 29.4 %reduce-scatter.2.cloned.1.call-done = f32[256,4,32]{0,2,1:T(8,128)} async-done(((f32[256,4,256]{0,2,1:T(8,128)}), f32[256,4,32]{0,2,1:T(8,128)}) %reduce-scatter.2.cloned.1.call-update) | async-done | bytes 131088 | tf_op jit(solution)/shard_map/reduce_scatter | solution.py:112
  120.7 2.0 fusion.33
  122.8 1.4 copy.63
  124.2 1.4 reshape.1541
  125.6 16.2 %all-to-all-start.2 = ((f32[64,1,1024]{2,1,0:T(1,128)}), f32[64,1,1024]{2,1,0:T(1,128)}, u32[]{:S(2)}, u32[]{:S(2)}) async-start(f32[64,1,1024]{2,1,0:T(1,128)} %reshape.1541), calls=%async_computation.3 | async-start | bytes 524288 | tf_op jit(solution)/shard_map/all_to_all | solution.py:114
  142.8 1.2 fusion.35
  144.1 1.3 pad_maximum_fusion.1
  145.5 15.2 %all-to-all-done.2 = f32[64,1,1024]{2,1,0:T(1,128)} async-done(((f32[64,1,1024]{2,1,0:T(1,128)}), f32[64,1,1024]{2,1,0:T(1,128)}, u32[]{:S(2)}, u32[]{:S(2)}) %all-to-all-start.2) | async-done | bytes 262176 | tf_op jit(solution)/shard_map/all_to_all | solution.py:114
  161.2 2.2 reduce.1
  163.4 1.5 reshape.1542
  164.9 1.4 copy.64
  167.6 2.0 convolution_bitcast_fusion.8
  169.6 1.3 copy.68
  170.8 3.0 reshape.1543
  173.8 4.5 all-to-all-start.3
  179.2 6.9 all-to-all-done.3
  186.0 2.2 reduce.2
  188.2 1.9 reshape.1544
  190.1 2.8 copy.151
  192.9 1.5 all_to_all.105
  194.5 1.9 fusion.9
  197.2 1.3 copy.73
  198.4 2.3 reshape.1545
  200.7 10.6 %all_to_all.126 = f32[8,1,8192]{2,1,0:T(1,128)} all-to-all(f32[8,1,8192]{2,1,0:T(1,128)S(1)} %reshape.1545), channel_id=1, replica_groups=mesh['band'=8,'pw'=64] {'band'}, dimensions={0} | all-to-all | bytes 524288 | tf_op jit(solution)/shard_map/all_to_all | solution.py:120
  211.3 6.1 all-to-all-start.6
  217.5 2.2 reduce.3
  219.7 1.9 reshape.1546
  221.6 2.8 copy.150
  224.4 1.5 reshape.1535
  226.0 1.4 convolution_bitcast_fusion.5
  227.4 1.6 copy.76
  229.0 1.8 reshape.1547
  231.0 14.9 %all-to-all-start.5 = ((f32[64,1,1024]{2,1,0:T(1,128)}), f32[64,1,1024]{2,1,0:T(1,128)S(1)}, u32[]{:S(2)}, u32[]{:S(2)}) async-start(f32[64,1,1024]{2,1,0:T(1,128)} %reshape.1547), calls=%async_computation.6 | async-start | bytes 524288 | tf_op jit(solution)/shard_map/all_to_all | solution.py:122
  245.9 1.6 copy.56
  248.8 2.8 fusion.3
  251.6 2.3 copy.58
  253.8 12.9 %all-to-all-done.5 = f32[64,1,1024]{2,1,0:T(1,128)S(1)} async-done(((f32[64,1,1024]{2,1,0:T(1,128)}), f32[64,1,1024]{2,1,0:T(1,128)S(1)}, u32[]{:S(2)}, u32[]{:S(2)}) %all-to-all-start.5) | async-done | bytes 262176 | tf_op jit(solution)/shard_map/all_to_all | solution.py:122
  266.7 6.2 all-to-all-start.1
  273.3 1.3 reduce.4
  276.9 2.4 fusion.11
  279.3 30.2 %all-gather.3.cloned.1.call-done = f32[1,256,4,256]{1,3,2,0:T(8,128)} async-done(((f32[1,256,4,32]{1,3,2,0:T(8,128)}), f32[1,256,4,256]{1,3,2,0:T(8,128)}) %all-gather.3.cloned.1.call-update) | async-done | bytes 1048592 | tf_op jit(solution)/shard_map/all_gather | solution.py:124
  310.5 2.4 collective-permute-start
  312.9 1.5 fusion.96
  314.4 1.5 fusion.94
  315.9 6.3 collective-permute-done
  322.2 1.3 pad_maximum_fusion
  323.6 1.1 copy.80
  324.9 45.7 %gather_fusion.7 = f32[8192]{0:T(1024)S(1)} fusion(f32[327680]{0:T(1024)S(1)} %reshape.1420, s32[8192]{0:T(1024)} %get-tuple-element.8), kind=kCustom, calls=%fused_computation.7 | custom fusion | bytes 98304 | tf_op jit(solution)/shard_map/gather | solution.py:141
  370.6 45.5 %gather_fusion.6 = f32[8192]{0:T(1024)S(1)} fusion(f32[327680]{0:T(1024)S(1)} %reshape.1420, s32[8192]{0:T(1024)S(1)} %copy-done.18), kind=kCustom, calls=%fused_computation.6 | custom fusion | bytes 98304 | tf_op jit(solution)/shard_map/gather | solution.py:141
  416.2 45.5 %gather_fusion.5 = f32[8192]{0:T(1024)S(1)} fusion(f32[327680]{0:T(1024)S(1)} %reshape.1420, s32[8192]{0:T(1024)S(1)} %copy-done.17), kind=kCustom, calls=%fused_computation.5 | custom fusion | bytes 98304 | tf_op jit(solution)/shard_map/gather | solution.py:141
  461.7 45.5 %gather_fusion.4 = f32[8192]{0:T(1024)S(1)} fusion(f32[327680]{0:T(1024)S(1)} %reshape.1420, s32[8192]{0:T(1024)S(1)} %copy-done.16), kind=kCustom, calls=%fused_computation.4 | custom fusion | bytes 98304 | tf_op jit(solution)/shard_map/gather | solution.py:141
  507.3 45.5 %gather_fusion.3 = f32[8192]{0:T(1024)S(1)} fusion(f32[327680]{0:T(1024)S(1)} %reshape.1420, s32[8192]{0:T(1024)S(1)} %copy-done.12), kind=kCustom, calls=%fused_computation.3 | custom fusion | bytes 98304 | tf_op jit(solution)/shard_map/gather | solution.py:141
  552.9 45.5 %gather_fusion.2 = f32[8192]{0:T(1024)S(1)} fusion(f32[327680]{0:T(1024)S(1)} %reshape.1420, s32[8192]{0:T(1024)S(1)} %copy-done.15), kind=kCustom, calls=%fused_computation.2 | custom fusion | bytes 98304 | tf_op jit(solution)/shard_map/gather | solution.py:141
  598.4 45.5 %gather_fusion.1 = f32[8192]{0:T(1024)S(1)} fusion(f32[327680]{0:T(1024)S(1)} %reshape.1420, s32[8192]{0:T(1024)S(1)} %copy-done.14), kind=kCustom, calls=%fused_computation.1 | custom fusion | bytes 98304 | tf_op jit(solution)/shard_map/gather | solution.py:141
  644.0 45.5 %gather_fusion = f32[8192]{0:T(1024)S(1)} fusion(f32[327680]{0:T(1024)S(1)} %reshape.1420, s32[8192]{0:T(1024)S(1)} %copy-done.13), kind=kCustom, calls=%fused_computation | custom fusion | bytes 98304 | tf_op jit(solution)/shard_map/gather | solution.py:141
  690.6 16.6 %all-to-all-start.7 = ((f32[8,64,1,128]{3,0,2,1:T(8,128)}), f32[8,64,1,128]{3,0,2,1:T(8,128)S(1)}, u32[]{:S(2)}, u32[]{:S(2)}) async-start(f32[8,64,1,128]{3,0,2,1:T(8,128)} %stack.131), calls=%async_computation.8 | async-start | bytes 524288 | tf_op jit(solution)/shard_map/all_to_all | solution.py:143
  707.2 1.5 copy.59
  709.7 1.8 convolution_bitcast_fusion.2
  713.3 15.0 %all-to-all-done.7 = f32[8,64,1,128]{3,0,2,1:T(8,128)S(1)} async-done(((f32[8,64,1,128]{3,0,2,1:T(8,128)}), f32[8,64,1,128]{3,0,2,1:T(8,128)S(1)}, u32[]{:S(2)}, u32[]{:S(2)}) %all-to-all-start.7) | async-done | bytes 262176 | tf_op jit(solution)/shard_map/all_to_all | solution.py:143
  (79 shorter events, 20.4 us)
Async XLA Ops:
  7.2 1.5 copy-start.11
  11.6 73.9 %all-to-all-start = ((f32[1,2,2,256,256]{4,1,2,0,3:T(2,128)}), f32[1,2,2,256,256]{4,1,2,0,3:T(2,128)S(1)}, u32[]{:S(2)}, u32[]{:S(2)}) async-start(f32[1,2,2,256,256]{4,1,2,0,3:T(2,128)} %copy.52), calls=%async_computation | async-start | bytes 2097152 | tf_op jit(solution)/shard_map/all_to_all | solution.py:88
  30.4 90.4 %reduce-scatter.2.cloned.1.call-start = ((), (), s32[]{:S(2)}) async-start(), calls=%async_computation.9 | async-start | bytes 1179648 | tf_op jit(solution)/shard_map/reduce_scatter | solution.py:112
  91.4 29.4 %copy-start.9 = (f32[256,1,256]{2,0,1:T(8,128)}, f32[256,1,256]{2,0,1:T(8,128)S(1)}, u32[]{:S(2)}) copy-start(f32[256,1,256]{2,0,1:T(8,128)S(1)} %fusion.57) | copy-start | bytes 786436
  125.6 35.1 %all-to-all-start.2 = ((f32[64,1,1024]{2,1,0:T(1,128)}), f32[64,1,1024]{2,1,0:T(1,128)}, u32[]{:S(2)}, u32[]{:S(2)}) async-start(f32[64,1,1024]{2,1,0:T(1,128)} %reshape.1541), calls=%async_computation.3 | async-start | bytes 524288 | tf_op jit(solution)/shard_map/all_to_all | solution.py:114
  144.0 1.3 copy-start.1
  144.1 1.4 copy-start.3
  166.4 1.2 copy-start
  173.8 12.2 %all-to-all-start.3 = ((f32[8,1,8192]{2,1,0:T(1,128)}), f32[8,1,8192]{2,1,0:T(1,128)}, u32[]{:S(2)}, u32[]{:S(2)}) async-start(f32[8,1,8192]{2,1,0:T(1,128)} %reshape.1543), calls=%async_computation.4 | async-start | bytes 524288 | tf_op jit(solution)/shard_map/all_to_all | solution.py:116
  211.3 19.6 %all-to-all-start.6 = ((s32[1,64,128]{2,0,1:T(1,128)}), s32[1,64,128]{2,0,1:T(1,128)}, u32[]{:S(2)}, u32[]{:S(2)}) async-start(s32[1,64,128]{2,0,1:T(1,128)} %bitcast.297), calls=%async_computation.7 | async-start | bytes 65536 | tf_op jit(solution)/shard_map/all_to_all | solution.py:129
  231.0 35.8 %all-to-all-start.5 = ((f32[64,1,1024]{2,1,0:T(1,128)}), f32[64,1,1024]{2,1,0:T(1,128)S(1)}, u32[]{:S(2)}, u32[]{:S(2)}) async-start(f32[64,1,1024]{2,1,0:T(1,128)} %reshape.1547), calls=%async_computation.6 | async-start | bytes 524288 | tf_op jit(solution)/shard_map/all_to_all | solution.py:122
  248.0 0.7 copy-start.5
  248.0 0.8 copy-start.7
  266.7 423.9 %all-to-all-start.1 = ((f32[1,2,128,4,256]{4,1,3,0,2:T(2,128)}), f32[1,2,128,4,256]{4,1,3,0,2:T(2,128)}, u32[]{:S(2)}, u32[]{:S(2)}) async-start(f32[1,2,128,4,256]{4,1,3,0,2:T(2,128)} %copy.58), calls=%async_computation.1 | async-start | bytes 2097152 | tf_op jit(solution)/shard_map/all_to_all | solution.py:98
  273.0 36.5 %all-gather.3.cloned.1.call-start = ((), (), s32[]{:S(2)}) async-start(), calls=%async_computation.10 | async-start | bytes 1179648 | tf_op jit(solution)/shard_map/all_gather | solution.py:124
  275.7 1.0 copy-start.2
  275.7 1.2 copy-start.4
  310.5 11.8 %collective-permute-start = (f32[256,1,256]{0,2,1:T(8,128)S(1)}, f32[256,1,256]{0,2,1:T(8,128)S(1)}, u32[]{:S(2)}, u32[]{:S(2)}) collective-permute-start(f32[256,1,256]{0,2,1:T(8,128)S(1)} %slice.36), channel_id=1, source_target_pairs={{0,63},{1,0},{2,1},{3,2},{4,3},{5,4},{6,5},{7,6},{8,7},{9,8},{10,9... | collective-permute-start | bytes 786440 | tf_op jit(solution)/shard_map/ppermute | solution.py:14
  324.9 45.7 %copy-start.18 = (s32[8192]{0:T(1024)S(1)}, s32[8192]{0:T(1024)}, u32[]{:S(2)}) copy-start(s32[8192]{0:T(1024)} %get-tuple-element.22) | copy-start | bytes 98308
  370.6 45.6 %copy-start.17 = (s32[8192]{0:T(1024)S(1)}, s32[8192]{0:T(1024)}, u32[]{:S(2)}) copy-start(s32[8192]{0:T(1024)} %get-tuple-element.23) | copy-start | bytes 98308
  416.2 45.6 %copy-start.16 = (s32[8192]{0:T(1024)S(1)}, s32[8192]{0:T(1024)}, u32[]{:S(2)}) copy-start(s32[8192]{0:T(1024)} %get-tuple-element.24) | copy-start | bytes 98308
  461.7 45.6 %copy-start.12 = (s32[8192]{0:T(1024)S(1)}, s32[8192]{0:T(1024)}, u32[]{:S(2)}) copy-start(s32[8192]{0:T(1024)} %get-tuple-element.31) | copy-start | bytes 98308
  507.3 45.6 %copy-start.15 = (s32[8192]{0:T(1024)S(1)}, s32[8192]{0:T(1024)}, u32[]{:S(2)}) copy-start(s32[8192]{0:T(1024)} %get-tuple-element.30) | copy-start | bytes 98308
  552.8 45.6 %copy-start.14 = (s32[8192]{0:T(1024)S(1)}, s32[8192]{0:T(1024)}, u32[]{:S(2)}) copy-start(s32[8192]{0:T(1024)} %get-tuple-element.29) | copy-start | bytes 98308
  598.4 45.6 %copy-start.13 = (s32[8192]{0:T(1024)S(1)}, s32[8192]{0:T(1024)}, u32[]{:S(2)}) copy-start(s32[8192]{0:T(1024)} %get-tuple-element.28) | copy-start | bytes 98308
  690.6 37.7 %all-to-all-start.7 = ((f32[8,64,1,128]{3,0,2,1:T(8,128)}), f32[8,64,1,128]{3,0,2,1:T(8,128)S(1)}, u32[]{:S(2)}, u32[]{:S(2)}) async-start(f32[8,64,1,128]{3,0,2,1:T(8,128)} %stack.131), calls=%async_computation.8 | async-start | bytes 524288 | tf_op jit(solution)/shard_map/all_to_all | solution.py:143
  708.7 1.0 copy-start.6
  708.7 1.0 copy-start.8
  711.5 16.8 %copy-start.10 = (f32[8,1,64,128]{3,2,1,0:T(8,128)S(1)}, f32[8,1,64,128]{3,2,1,0:T(8,128)}, u32[]{:S(2)}) copy-start(f32[8,1,64,128]{3,2,1,0:T(8,128)} %param.12) | copy-start | bytes 786436
  711.5 17.0 %copy-start.19 = (s32[1,64]{1,0:T(1,128)S(1)}, s32[1,64]{1,0:T(1,128)}, u32[]{:S(2)}) copy-start(s32[1,64]{1,0:T(1,128)} %param.13) | copy-start | bytes 772
Sparse Core Ops, SparseCore 0:
  89.5 31.1 reduce-scatter.1
  279.4 29.9 all-gather.2
where the time goes:
time: 746 us; the launch traced here: 737 us
  local copies, waits for them, and re-layouts  411 us (55%)
  waiting for transfers between devices  170 us (23%)
  starting transfers between devices  86.1 us (12%)
  other arithmetic  22.6 us (3%)
  matrix products  19.7 us (3%)
  between operations  15.8 us (2%)
  blocking collectives  10.6 us (1%)
    gather x8, local copies, waits for them, and re-layouts, body(): gathered.append(flattened[cell_index])  364 us
    all_to_all x1, waiting for transfers between devices, body(): lax.all_to_all(partial_section, 'pw', split_axis=3, concat_axis=2, tiled=...  54.5 us
    all_gather x1, waiting for transfers between devices, body(): hartree = lax.all_gather(hartree_part, 'band', axis=2, tiled=True)  30.2 us
    reduce_scatter x1, waiting for transfers between devices, body(): lax.psum_scatter(partial_density, 'band', scatter_dimension=2, tiled=True)  29.4 us
    dot_general x12, matrix products, transform(): lax.dot_general(operand, matrix, (((component_axis, target_axis), (0, 1))...  19.7 us
    unnamed x50, local copies, waits for them, and re-layouts  19.3 us
    all_to_all x1, starting transfers between devices, body(): lax.all_to_all(partial_section, 'pw', split_axis=3, concat_axis=2, tiled=...  18.7 us
    all_to_all x1, starting transfers between devices, body(): lax.all_to_all(stacked, 'pw', split_axis=1, concat_axis=2, tiled=True)  16.6 us
  transfers between devices with their start and end apart: 10, of which 9 were waited for; matrix products, arithmetic and copies ran while one was open for 56% of the time, Pallas kernels for 0%

commit v1 on v0

--- a/solution.py
+++ b/solution.py
@@ -121,7 +121,12 @@
     spectrum = transform(spectrum, inverse_grid, 2, 0)
     spectrum = lax.all_to_all(spectrum, "pw", split_axis=2, concat_axis=1, tiled=True)
     hartree_part = transform(spectrum, inverse_grid[:, :, 0:1], 1, 0)[0] * inverse_norm
-    hartree = lax.all_gather(hartree_part, "band", axis=2, tiled=True)
+    ring = [hartree_part]
+    for hop in range(7):
+        ring.append(lax.ppermute(ring[-1], "band", [(dev, (dev + 1) % 8) for dev in range(8)]))
+    hartree = jnp.roll(
+        jnp.concatenate(ring[::-1], axis=2), (lax.axis_index("band") + 1) * ring[0].shape[2], axis=2
+    )
     upper_plane = shifted(hartree[:, 0:1, :], "pw", -1)
     extended = jnp.concatenate([hartree, upper_plane], axis=1)
     flattened = extended.reshape(-1)

time: 746 us -> 757 us (1.015)
    ppermute x0 -> x7, waiting for transfers between devices: none -> 37.6 us  [body(): lax.ppermute(ring[-1], 'band', [(dev, (dev + 1) % 8) for dev in range(8)])]
    all_gather x1 -> x0, waiting for transfers between devices: 30.2 us -> none  [body(): hartree = lax.all_gather(hartree_part, 'band', axis=2, tiled=True)]
    unnamed x50 -> x83, local copies, waits for them, and re-layouts: 19.3 us -> 23.8 us
  transfers between devices with their start and end apart: 10 -> 16, of which waited for: 9 -> 15; matrix products, arithmetic and copies ran while one was open for 56% -> 55% of each run, Pallas kernels for 0% -> 0%
where the time goes in v1:
time: 757 us; the launch traced here: 747 us
  local copies, waits for them, and re-layouts  416 us (55%)
  waiting for transfers between devices  176 us (23%)
  starting transfers between devices  86.2 us (11%)
  other arithmetic  22.4 us (3%)
  matrix products  20 us (3%)
  between operations  16 us (2%)
  blocking collectives  10.6 us (1%)
    gather x8, local copies, waits for them, and re-layouts, body(): gathered.append(flattened[cell_index])  364 us
    all_to_all x1, waiting for transfers between devices, body(): lax.all_to_all(partial_section, 'pw', split_axis=3, concat_axis=2, tiled=...  54.5 us
    ppermute x7, waiting for transfers between devices, body(): lax.ppermute(ring[-1], 'band', [(dev, (dev + 1) % 8) for dev in range(8)])  37.6 us
    reduce_scatter x1, waiting for transfers between devices, body(): lax.psum_scatter(partial_density, 'band', scatter_dimension=2, tiled=True)  29.3 us
    unnamed x83, local copies, waits for them, and re-layouts  23.8 us
    dot_general x12, matrix products, transform(): lax.dot_general(operand, matrix, (((component_axis, target_axis), (0, 1))...  20 us
    all_to_all x1, starting transfers between devices, body(): lax.all_to_all(partial_section, 'pw', split_axis=3, concat_axis=2, tiled=...  18.7 us
    all_to_all x1, starting transfers between devices, body(): lax.all_to_all(stacked, 'pw', split_axis=1, concat_axis=2, tiled=True)  17.6 us
  transfers between devices with their start and end apart: 16, of which 15 were waited for; matrix products, arithmetic and copies ran while one was open for 55% of the time, Pallas kernels for 0%

profile of v1, /device:TPU:8, one launch (start us, length us, event | category | flops | bytes accessed | tf_op | source)
XLA Modules:
  0.0 747.0 jit_solution(2600966711890709063)
XLA Ops:
  7.8 1.4 compare_select_fusion
  9.3 1.6 convolution_bitcast_fusion.3
  13.2 18.7 %all-to-all-start = ((f32[1,2,2,256,256]{4,1,2,0,3:T(2,128)}), f32[1,2,2,256,256]{4,1,2,0,3:T(2,128)S(1)}, u32[]{:S(2)}, u32[]{:S(2)}) async-start(f32[1,2,2,256,256]{4,1,2,0,3:T(2,128)} %copy.52), calls=%async_computation | async-start | bytes 2097152 | tf_op jit(solution)/shard_map/all_to_all | solution.py:88
  32.7 54.5 %all-to-all-done = f32[1,2,2,256,256]{4,1,2,0,3:T(2,128)S(1)} async-done(((f32[1,2,2,256,256]{4,1,2,0,3:T(2,128)}), f32[1,2,2,256,256]{4,1,2,0,3:T(2,128)S(1)}, u32[]{:S(2)}, u32[]{:S(2)}) %all-to-all-start) | async-done | bytes 1048608 | tf_op jit(solution)/shard_map/all_to_all | solution.py:88
  88.0 1.9 convolution_bitcast_fusion
  93.0 29.3 %reduce-scatter.2.cloned.1.call-done = f32[256,4,32]{0,2,1:T(8,128)} async-done(((f32[256,4,256]{0,2,1:T(8,128)}), f32[256,4,32]{0,2,1:T(8,128)}) %reduce-scatter.2.cloned.1.call-update) | async-done | bytes 131088 | tf_op jit(solution)/shard_map/reduce_scatter | solution.py:112
  122.3 2.1 fusion.33
  124.4 1.4 copy.63
  125.8 1.4 reshape.1540
  127.2 16.3 %all-to-all-start.2 = ((f32[64,1,1024]{2,1,0:T(1,128)}), f32[64,1,1024]{2,1,0:T(1,128)}, u32[]{:S(2)}, u32[]{:S(2)}) async-start(f32[64,1,1024]{2,1,0:T(1,128)} %reshape.1540), calls=%async_computation.3 | async-start | bytes 524288 | tf_op jit(solution)/shard_map/all_to_all | solution.py:114
  147.2 15.3 %all-to-all-done.2 = f32[64,1,1024]{2,1,0:T(1,128)} async-done(((f32[64,1,1024]{2,1,0:T(1,128)}), f32[64,1,1024]{2,1,0:T(1,128)}, u32[]{:S(2)}, u32[]{:S(2)}) %all-to-all-start.2) | async-done | bytes 262176 | tf_op jit(solution)/shard_map/all_to_all | solution.py:114
  163.0 2.2 reduce.1
  165.2 1.5 reshape.1541
  166.7 1.5 copy.64
  169.0 2.0 convolution_bitcast_fusion.8
  172.2 3.0 reshape.1542
  175.2 4.0 all-to-all-start.3
  179.4 7.4 all-to-all-done.3
  186.8 2.2 reduce.2
  189.0 1.9 reshape.1543
  190.9 2.8 copy.151
  193.7 1.5 all_to_all.105
  195.2 1.9 fusion.9
  199.2 2.3 reshape.1544
  201.5 10.6 %all_to_all.126 = f32[8,1,8192]{2,1,0:T(1,128)} all-to-all(f32[8,1,8192]{2,1,0:T(1,128)S(1)} %reshape.1544), channel_id=1, replica_groups=mesh['band'=8,'pw'=64] {'band'}, dimensions={0} | all-to-all | bytes 524288 | tf_op jit(solution)/shard_map/all_to_all | solution.py:120
  212.1 6.5 all-to-all-start.6
  218.6 2.2 reduce.3
  220.8 1.9 reshape.1545
  222.7 2.8 copy.150
  225.5 1.5 reshape.1534
  227.0 1.4 convolution_bitcast_fusion.5
  228.4 1.6 copy.76
  230.1 1.8 reshape.1546
  232.3 14.8 %all-to-all-start.5 = ((f32[64,1,1024]{2,1,0:T(1,128)}), f32[64,1,1024]{2,1,0:T(1,128)}, u32[]{:S(2)}, u32[]{:S(2)}) async-start(f32[64,1,1024]{2,1,0:T(1,128)} %reshape.1546), calls=%async_computation.6 | async-start | bytes 524288 | tf_op jit(solution)/shard_map/all_to_all | solution.py:122
  247.1 1.6 copy.56
  250.0 2.8 fusion.3
  252.8 2.3 copy.58
  255.1 12.8 %all-to-all-done.5 = f32[64,1,1024]{2,1,0:T(1,128)} async-done(((f32[64,1,1024]{2,1,0:T(1,128)}), f32[64,1,1024]{2,1,0:T(1,128)}, u32[]{:S(2)}, u32[]{:S(2)}) %all-to-all-start.5) | async-done | bytes 262176 | tf_op jit(solution)/shard_map/all_to_all | solution.py:122
  267.9 6.0 all-to-all-start.1
  273.9 2.2 reduce.4
  278.2 1.8 fusion.11
  280.1 5.6 collective-permute-done
  285.6 5.6 collective-permute-done.1
  291.3 5.6 collective-permute-done.2
  296.9 5.6 collective-permute-done.3
  302.5 5.6 collective-permute-done.4
  308.1 5.6 collective-permute-done.5
  313.7 1.5 fusion.96
  315.2 4.0 collective-permute-done.6
  325.2 2.2 collective-permute-start.7
  328.3 5.2 collective-permute-done.7
  333.6 1.9 copy.80
  335.5 1.6 reshape.1420
  337.2 45.5 %gather_fusion.7 = f32[8192]{0:T(1024)S(1)} fusion(f32[327680]{0:T(1024)S(1)} %reshape.1420, s32[8192]{0:T(1024)S(1)} %copy-done.25), kind=kCustom, calls=%fused_computation.7 | custom fusion | bytes 98304 | tf_op jit(solution)/shard_map/gather | solution.py:146
  382.7 45.5 %gather_fusion.6 = f32[8192]{0:T(1024)S(1)} fusion(f32[327680]{0:T(1024)S(1)} %reshape.1420, s32[8192]{0:T(1024)S(1)} %copy-done.27), kind=kCustom, calls=%fused_computation.6 | custom fusion | bytes 98304 | tf_op jit(solution)/shard_map/gather | solution.py:146
  428.3 45.5 %gather_fusion.5 = f32[8192]{0:T(1024)S(1)} fusion(f32[327680]{0:T(1024)S(1)} %reshape.1420, s32[8192]{0:T(1024)S(1)} %copy-done.26), kind=kCustom, calls=%fused_computation.5 | custom fusion | bytes 98304 | tf_op jit(solution)/shard_map/gather | solution.py:146
  473.8 45.5 %gather_fusion.4 = f32[8192]{0:T(1024)S(1)} fusion(f32[327680]{0:T(1024)S(1)} %reshape.1420, s32[8192]{0:T(1024)S(1)} %get-tuple-element.24), kind=kCustom, calls=%fused_computation.4 | custom fusion | bytes 98304 | tf_op jit(solution)/shard_map/gather | solution.py:146
  519.4 45.5 %gather_fusion.3 = f32[8192]{0:T(1024)S(1)} fusion(f32[327680]{0:T(1024)S(1)} %reshape.1420, s32[8192]{0:T(1024)S(1)} %copy-done.24), kind=kCustom, calls=%fused_computation.3 | custom fusion | bytes 98304 | tf_op jit(solution)/shard_map/gather | solution.py:146
  564.9 45.5 %gather_fusion.2 = f32[8192]{0:T(1024)S(1)} fusion(f32[327680]{0:T(1024)S(1)} %reshape.1420, s32[8192]{0:T(1024)S(1)} %get-tuple-element.30), kind=kCustom, calls=%fused_computation.2 | custom fusion | bytes 98304 | tf_op jit(solution)/shard_map/gather | solution.py:146
  610.5 45.5 %gather_fusion.1 = f32[8192]{0:T(1024)S(1)} fusion(f32[327680]{0:T(1024)S(1)} %reshape.1420, s32[8192]{0:T(1024)S(1)} %get-tuple-element.29), kind=kCustom, calls=%fused_computation.1 | custom fusion | bytes 98304 | tf_op jit(solution)/shard_map/gather | solution.py:146
  656.0 45.5 %gather_fusion = f32[8192]{0:T(1024)S(1)} fusion(f32[327680]{0:T(1024)S(1)} %reshape.1420, s32[8192]{0:T(1024)S(1)} %get-tuple-element.28), kind=kCustom, calls=%fused_computation | custom fusion | bytes 98304 | tf_op jit(solution)/shard_map/gather | solution.py:146
  702.6 17.6 %all-to-all-start.7 = ((f32[8,64,1,128]{3,0,2,1:T(8,128)}), f32[8,64,1,128]{3,0,2,1:T(8,128)}, u32[]{:S(2)}, u32[]{:S(2)}) async-start(f32[8,64,1,128]{3,0,2,1:T(8,128)} %stack.131), calls=%async_computation.8 | async-start | bytes 524288 | tf_op jit(solution)/shard_map/all_to_all | solution.py:148
  721.2 1.8 convolution_bitcast_fusion.2
  724.7 13.1 %all-to-all-done.7 = f32[8,64,1,128]{3,0,2,1:T(8,128)} async-done(((f32[8,64,1,128]{3,0,2,1:T(8,128)}), f32[8,64,1,128]{3,0,2,1:T(8,128)}, u32[]{:S(2)}, u32[]{:S(2)}) %all-to-all-start.7) | async-done | bytes 262176 | tf_op jit(solution)/shard_map/all_to_all | solution.py:148
  (125 shorter events, 31.3 us)
Async XLA Ops:
  13.2 73.9 %all-to-all-start = ((f32[1,2,2,256,256]{4,1,2,0,3:T(2,128)}), f32[1,2,2,256,256]{4,1,2,0,3:T(2,128)S(1)}, u32[]{:S(2)}, u32[]{:S(2)}) async-start(f32[1,2,2,256,256]{4,1,2,0,3:T(2,128)} %copy.52), calls=%async_computation | async-start | bytes 2097152 | tf_op jit(solution)/shard_map/all_to_all | solution.py:88
  32.0 90.4 %reduce-scatter.2.cloned.1.call-start = ((), (), s32[]{:S(2)}) async-start(), calls=%async_computation.9 | async-start | bytes 1179648 | tf_op jit(solution)/shard_map/reduce_scatter | solution.py:112
  93.0 29.3 %copy-start.7 = (f32[256,1,256]{2,0,1:T(8,128)}, f32[256,1,256]{2,0,1:T(8,128)S(1)}, u32[]{:S(2)}) copy-start(f32[256,1,256]{2,0,1:T(8,128)S(1)} %fusion.57) | copy-start | bytes 786436
  127.2 35.3 %all-to-all-start.2 = ((f32[64,1,1024]{2,1,0:T(1,128)}), f32[64,1,1024]{2,1,0:T(1,128)}, u32[]{:S(2)}, u32[]{:S(2)}) async-start(f32[64,1,1024]{2,1,0:T(1,128)} %reshape.1540), calls=%async_computation.3 | async-start | bytes 524288 | tf_op jit(solution)/shard_map/all_to_all | solution.py:114
  145.7 1.3 copy-start.1
  145.8 1.3 copy-start.3
  166.7 2.2 copy-start
  175.2 11.6 %all-to-all-start.3 = ((f32[8,1,8192]{2,1,0:T(1,128)}), f32[8,1,8192]{2,1,0:T(1,128)}, u32[]{:S(2)}, u32[]{:S(2)}) async-start(f32[8,1,8192]{2,1,0:T(1,128)} %reshape.1542), calls=%async_computation.4 | async-start | bytes 524288 | tf_op jit(solution)/shard_map/all_to_all | solution.py:116
  212.1 20.2 %all-to-all-start.6 = ((s32[1,64,128]{2,0,1:T(1,128)}), s32[1,64,128]{2,0,1:T(1,128)S(1)}, u32[]{:S(2)}, u32[]{:S(2)}) async-start(s32[1,64,128]{2,0,1:T(1,128)} %bitcast.98), calls=%async_computation.7 | async-start | bytes 65536 | tf_op jit(solution)/shard_map/all_to_all | solution.py:134
  232.3 20.5 %copy-start.21 = (s32[1,64,128]{2,0,1:T(1,128)}, s32[1,64,128]{2,0,1:T(1,128)S(1)}, u32[]{:S(2)}) copy-start(s32[1,64,128]{2,0,1:T(1,128)S(1)} %all-to-all-done.6) | copy-start | bytes 98308
  232.3 35.6 %all-to-all-start.5 = ((f32[64,1,1024]{2,1,0:T(1,128)}), f32[64,1,1024]{2,1,0:T(1,128)}, u32[]{:S(2)}, u32[]{:S(2)}) async-start(f32[64,1,1024]{2,1,0:T(1,128)} %reshape.1546), calls=%async_computation.6 | async-start | bytes 524288 | tf_op jit(solution)/shard_map/all_to_all | solution.py:122
  249.3 0.7 copy-start.5
  267.9 434.7 %all-to-all-start.1 = ((f32[1,2,128,4,256]{4,1,3,0,2:T(2,128)}), f32[1,2,128,4,256]{4,1,3,0,2:T(2,128)S(1)}, u32[]{:S(2)}, u32[]{:S(2)}) async-start(f32[1,2,128,4,256]{4,1,3,0,2:T(2,128)} %copy.58), calls=%async_computation.1 | async-start | bytes 2097152 | tf_op jit(solution)/shard_map/all_to_all | solution.py:98
  277.0 1.0 copy-start.2
  277.0 1.2 copy-start.4
  280.0 5.6 collective-permute-start
  285.6 29.6 %copy-start.8 = (f32[256,4,32]{0,2,1:T(8,128)}, f32[256,4,32]{0,2,1:T(8,128)S(1)}, u32[]{:S(2)}) copy-start(f32[256,4,32]{0,2,1:T(8,128)S(1)} %collective-permute-done) | copy-start | bytes 393220
  285.6 5.6 collective-permute-start.1
  291.2 24.0 %copy-start.10 = (f32[256,4,32]{0,2,1:T(8,128)}, f32[256,4,32]{0,2,1:T(8,128)S(1)}, u32[]{:S(2)}) copy-start(f32[256,4,32]{0,2,1:T(8,128)S(1)} %collective-permute-done.1) | copy-start | bytes 393220
  291.2 5.6 collective-permute-start.2
  296.9 18.3 %copy-start.12 = (f32[256,4,32]{0,2,1:T(8,128)}, f32[256,4,32]{0,2,1:T(8,128)S(1)}, u32[]{:S(2)}) copy-start(f32[256,4,32]{0,2,1:T(8,128)S(1)} %collective-permute-done.2) | copy-start | bytes 393220
  296.9 5.6 collective-permute-start.3
  302.5 12.7 %copy-start.14 = (f32[256,4,32]{0,2,1:T(8,128)}, f32[256,4,32]{0,2,1:T(8,128)S(1)}, u32[]{:S(2)}) copy-start(f32[256,4,32]{0,2,1:T(8,128)S(1)} %collective-permute-done.3) | copy-start | bytes 393220
  302.5 5.6 collective-permute-start.4
  308.1 7.2 copy-start.16
  308.1 5.6 collective-permute-start.5
  313.7 1.6 copy-start.18
  313.7 5.6 collective-permute-start.6
  319.3 5.7 copy-start.19
  319.3 5.7 copy-start.17
  319.3 5.7 copy-start.15
  319.3 5.8 copy-start.13
  319.3 5.8 copy-start.11
  319.3 5.8 copy-start.9
  320.3 7.1 copy-start.22
  325.2 8.3 %collective-permute-start.7 = (f32[256,1,256]{0,2,1:T(8,128)S(1)}, f32[256,1,256]{0,2,1:T(8,128)S(1)}, u32[]{:S(2)}, u32[]{:S(2)}) collective-permute-start(f32[256,1,256]{0,2,1:T(8,128)S(1)} %constant_dynamic-slice_fusion), channel_id=1, source_target_pairs={{0,63},{1,0},{2,1},{3,2},{4,3},{5,4},{6,5},{7,6},{8,7},{9,8},{10,9... | collective-permute-start | bytes 786440 | tf_op jit(solution)/shard_map/ppermute | solution.py:14
  335.5 1.7 copy-start.25
  337.1 45.6 %copy-start.27 = (s32[8192]{0:T(1024)S(1)}, s32[8192]{0:T(1024)}, u32[]{:S(2)}) copy-start(s32[8192]{0:T(1024)} %get-tuple-element.22) | copy-start | bytes 98308
  382.7 45.6 %copy-start.26 = (s32[8192]{0:T(1024)S(1)}, s32[8192]{0:T(1024)}, u32[]{:S(2)}) copy-start(s32[8192]{0:T(1024)} %get-tuple-element.23) | copy-start | bytes 98308
  473.8 45.6 %copy-start.24 = (s32[8192]{0:T(1024)S(1)}, s32[8192]{0:T(1024)}, u32[]{:S(2)}) copy-start(s32[8192]{0:T(1024)} %get-tuple-element.31) | copy-start | bytes 98308
  702.6 35.2 %all-to-all-start.7 = ((f32[8,64,1,128]{3,0,2,1:T(8,128)}), f32[8,64,1,128]{3,0,2,1:T(8,128)}, u32[]{:S(2)}, u32[]{:S(2)}) async-start(f32[8,64,1,128]{3,0,2,1:T(8,128)} %stack.131), calls=%async_computation.8 | async-start | bytes 524288 | tf_op jit(solution)/shard_map/all_to_all | solution.py:148
  720.2 1.0 copy-start.6
  720.5 2.5 copy-start.20
  721.1 16.7 %copy-start.23 = (f32[8,1,64,128]{3,2,1,0:T(8,128)S(1)}, f32[8,1,64,128]{3,2,1,0:T(8,128)}, u32[]{:S(2)}) copy-start(f32[8,1,64,128]{3,2,1,0:T(8,128)} %param.12) | copy-start | bytes 786436
  721.2 17.8 %copy-start.28 = (s32[1,64]{1,0:T(1,128)S(1)}, s32[1,64]{1,0:T(1,128)}, u32[]{:S(2)}) copy-start(s32[1,64]{1,0:T(1,128)} %param.13) | copy-start | bytes 772
Sparse Core Ops, SparseCore 0:
  91.1 31.1 reduce-scatter.1
